TPU v7x, 512 devices: a whole 4x8x8 slice. The times are simulated.
512 devices in a mesh: pair: 32 (over y_lo, z), day: 16 (over y_hi, x, core).
Axes of the slice: x: 4, y: 8 (y_hi: 2, y_lo: 4; y = y_hi * 4 + y_lo), z: 8, core: 2. Of those that a mesh axis runs over, the one named last changes fastest.
Arguments:
- spectra: bfloat16 [32, 2, 2048, 1024], P('day', None, 'pair'), may hold values from -6 to 6
- band_weights: float32 [8, 2048], replicated, may hold values from 0.05 to 1
- pair_stations: int32 [1536, 2], replicated, may hold values from 0 to 1023
- block_live: int32 [512], P(('pair', 'day')), may hold values from 1 to 3, 1152 in all
- windows: int32 [1536, 8, 2], P(('pair', 'day')), may hold values from 0 to 4096, as said below
- observed: bfloat16 [1536, 8, 4096], P(('pair', 'day')), may hold values from -6 to 6
Outputs:
- adjoint: float32 [32, 2, 2048, 1024], P('day', None, 'pair')
Inputs may be any that keep to these rules, and one draw needn't show every extreme that they name: Block b holds pairs b * 3 to b * 3 + 2, and its first block_live[b] pairs are live. windows[p, k, 0] < windows[p, k, 1].
All inputs are finite; a program needn't handle non-finite values.
Results may differ from a plain program's by a relative error of at most 0.0035.
Values sent between devices are 32-bit elements; how exact they have to be, the bound alone decides.
A program may use at most 64 MiB of HBM per device.

v0:
```python
import math
import jax
import jax.numpy as jnp
from jax import lax
from jax.sharding import PartitionSpec as P


def table_block(start, width, lags):
    half = lags // 2
    freqs = jnp.arange(half, dtype=jnp.int32)
    lag_index = start + jnp.arange(width, dtype=jnp.int32)
    phase = freqs[:, None] * lag_index[None, :] % lags
    angle = phase.astype(jnp.float32) * (2.0 * math.pi / lags)
    return jnp.concatenate([jnp.cos(angle), -jnp.sin(angle)], axis=0).astype(jnp.bfloat16)


def one_hot_rows(identity, columns):
    return (identity[:, None] == columns[None, :]).astype(jnp.bfloat16)


def gather_rows(flat_spectra, stations):
    count = stations.shape[0]
    station_count = flat_spectra.shape[1]
    width = math.gcd(count, 512)
    columns = jnp.arange(station_count, dtype=jnp.int32)
    dims = (((1,), (1,)), ((), ()))

    def gather_step(index, buffers):
        start = index * width
        identity = lax.dynamic_slice_in_dim(stations, start, width, 0)
        first_hot = one_hot_rows(identity[:, 0], columns)
        second_hot = one_hot_rows(identity[:, 1], columns)
        first_part = lax.dot_general(
            flat_spectra, first_hot, dims, preferred_element_type=jnp.float32
        ).astype(jnp.bfloat16)
        second_part = lax.dot_general(
            flat_spectra, second_hot, dims, preferred_element_type=jnp.float32
        ).astype(jnp.bfloat16)
        return (
            lax.dynamic_update_slice_in_dim(buffers[0], first_part, start, 1),
            lax.dynamic_update_slice_in_dim(buffers[1], second_part, start, 1),
        )

    empty = jnp.zeros((flat_spectra.shape[0], count), jnp.bfloat16)
    return lax.fori_loop(0, count // width, gather_step, (empty, empty))


def cross_stack(first_rows, second_rows, day_count, freq_count):
    count = first_rows.shape[1]
    first = first_rows.reshape(day_count, 2, freq_count, count).astype(jnp.float32)
    second = second_rows.reshape(day_count, 2, freq_count, count).astype(jnp.float32)
    real_part = jnp.sum(first[:, 0] * second[:, 0] + first[:, 1] * second[:, 1], axis=0)
    imag_part = jnp.sum(first[:, 0] * second[:, 1] - first[:, 1] * second[:, 0], axis=0)
    return jnp.stack([real_part, imag_part]).transpose(0, 2, 1)


def add_to_stations(accum, to_first, to_second, stations):
    count = stations.shape[0]
    station_count = accum.shape[1]
    width = math.gcd(count, 512)
    columns = jnp.arange(station_count, dtype=jnp.int32)

    def add_step(index, total):
        start = index * width
        identity = lax.dynamic_slice_in_dim(stations, start, width, 0)
        hot = jnp.concatenate(
            [one_hot_rows(identity[:, 0], columns), one_hot_rows(identity[:, 1], columns)], axis=0
        )
        terms = jnp.concatenate(
            [
                lax.dynamic_slice_in_dim(to_first, start, width, 1),
                lax.dynamic_slice_in_dim(to_second, start, width, 1),
            ],
            axis=1,
        )
        return total + jnp.dot(
            terms,
            hot.astype(jnp.float32),
            precision=lax.Precision.HIGHEST,
            preferred_element_type=jnp.float32,
        )

    return lax.fori_loop(0, count // width, add_step, accum)


def station_terms(accum, first_rows, second_rows, grads, stations, day_count):
    count = first_rows.shape[1]
    freq_count = grads.shape[2]
    first = first_rows.reshape(day_count, 2, freq_count, count).astype(jnp.float32)
    second = second_rows.reshape(day_count, 2, freq_count, count).astype(jnp.float32)
    turned = grads.transpose(0, 2, 1)
    grad_real = turned[0][None]
    grad_imag = turned[1][None]
    to_first = jnp.stack(
        [
            grad_real * second[:, 0] + grad_imag * second[:, 1],
            grad_real * second[:, 1] - grad_imag * second[:, 0],
        ],
        axis=1,
    ).reshape(-1, count)
    to_second = jnp.stack(
        [
            grad_real * first[:, 0] - grad_imag * first[:, 1],
            grad_real * first[:, 1] + grad_imag * first[:, 0],
        ],
        axis=1,
    ).reshape(-1, count)
    return add_to_stations(accum, to_first, to_second, stations)


def body(spectra, band_weights, pair_stations, block_live, windows, observed):
    n_pair = lax.axis_size("pair")
    n_day = lax.axis_size("day")
    per_block, bands, lags = observed.shape
    half = lags // 2
    day_count = spectra.shape[0]
    freq_count = spectra.shape[2]
    station_count = spectra.shape[3]
    days = day_count * n_day
    ordered = (
        pair_stations.reshape(n_pair, n_day, per_block, 2).transpose(1, 0, 2, 3).reshape(-1, 2)
    )
    flat_spectra = spectra.reshape(-1, station_count)
    first_rows, second_rows = gather_rows(flat_spectra, ordered)
    local_stack = cross_stack(first_rows, second_rows, day_count, freq_count)
    total = lax.psum(local_stack, "day")
    day_share = lax.dynamic_slice_in_dim(
        total, lax.axis_index("day") * (n_pair * per_block), n_pair * per_block, 1
    )
    pair_stack = lax.all_to_all(day_share, "pair", split_axis=1, concat_axis=2, tiled=True)
    weights_full = jnp.concatenate([band_weights, band_weights], axis=1)
    flat_stack = jnp.concatenate([pair_stack[0], pair_stack[1]], axis=1)
    weighted = (
        (flat_stack[:, None, :] * weights_full[None])
        .astype(jnp.bfloat16)
        .reshape(per_block * bands, lags)
    )
    live = jnp.arange(per_block, dtype=jnp.int32) < block_live[0]
    row_live = jnp.repeat(live, bands)
    lower_lag = windows[:, :, 0].reshape(-1)
    upper_lag = windows[:, :, 1].reshape(-1)
    observed_rows = observed.reshape(per_block * bands, lags)
    width = min(256, lags)
    forward_scale = 2.0 / math.sqrt(lags * days)
    adjoint_scale = 1.0 / math.sqrt(lags)

    def lag_step(index, accum):
        start = index * width
        block_table = table_block(start, width, lags)
        corr = forward_scale * jnp.dot(weighted, block_table, preferred_element_type=jnp.float32)
        lag_index = start + jnp.arange(width, dtype=jnp.int32)
        inside = (
            row_live[:, None]
            & (lag_index[None, :] >= lower_lag[:, None])
            & (lag_index[None, :] < upper_lag[:, None])
        )
        target = lax.dynamic_slice_in_dim(observed_rows, start, width, 1).astype(jnp.float32)
        misfit = jnp.where(inside, corr - target, 0.0).astype(jnp.bfloat16)
        return accum + lax.dot_general(
            misfit, block_table, (((1,), (1,)), ((), ())), preferred_element_type=jnp.float32
        )

    adjoint_rows = lax.fori_loop(
        0, lags // width, lag_step, jnp.zeros((per_block * bands, lags), jnp.float32)
    )
    summed = jnp.sum(adjoint_rows.reshape(per_block, bands, lags) * weights_full[None], axis=1)
    adjoint_spec = adjoint_scale * summed
    adjoint_split = adjoint_spec.reshape(per_block, 2, half).transpose(1, 0, 2)
    spread = lax.all_to_all(adjoint_split, "pair", split_axis=2, concat_axis=1, tiled=True)
    start_total = jnp.zeros((flat_spectra.shape[0], station_count), jnp.float32)
    all_pairs = lax.all_gather(spread, "day", axis=1, tiled=True)
    flat_out = station_terms(start_total, first_rows, second_rows, all_pairs, ordered, day_count)
    return flat_out.reshape(spectra.shape)


def solution(mesh):
    in_specs = (
        P("day", None, "pair", None),
        P(),
        P(),
        P(("pair", "day")),
        P(("pair", "day"), None, None),
        P(("pair", "day"), None, None),
    )
    out_specs = P("day", None, "pair", None)
    return jax.shard_map(body, mesh=mesh, in_specs=in_specs, out_specs=out_specs, check_vma=False)
```

profile of v0, /device:TPU:1, one launch (start us, length us, event | category | flops | bytes accessed | tf_op | source)
XLA Modules:
  0.0 495.4 jit_solution(16453960934737975883)
XLA Ops:
  8.3 4.5 while.49
  16.7 188.6 %all-reduce.2.cloned.1.call-done = f32[2,1536,64]{1,2,0:T(8,128)} async-done(((f32[2,1536,64]{1,2,0:T(8,128)}), f32[2,1536,64]{1,2,0:T(8,128)}) %all-reduce.2.cloned.1.call-update) | async-done | bytes 786448 | tf_op jit(solution)/shard_map/psum | solution.py:126
  207.2 7.7 %all-to-all-start = ((f32[32,1,384]{2,1,0:T(1,128)}), f32[32,1,384]{2,1,0:T(1,128)S(1)}, u32[]{:S(2)}, u32[]{:S(2)}) async-start(f32[32,1,384]{2,1,0:T(1,128)} %reshape.72), calls=%async_computation | async-start | bytes 98304 | tf_op jit(solution)/shard_map/all_to_all | solution.py:130
  214.9 9.1 %all-to-all-done = f32[32,1,384]{2,1,0:T(1,128)S(1)} async-done(((f32[32,1,384]{2,1,0:T(1,128)}), f32[32,1,384]{2,1,0:T(1,128)S(1)}, u32[]{:S(2)}, u32[]{:S(2)}) %all-to-all-start) | async-done | bytes 49184 | tf_op jit(solution)/shard_map/all_to_all | solution.py:130
  225.7 176.8 %while.51 = (s32[]{:T(128)}, f32[24,4096]{1,0:T(8,128)S(1)}, s32[3,8,1]{1,0,2:T(4,128)}, s32[3,8,1]{1,0,2:T(4,128)}, bf16[24,4096]{1,0:T(8,128)(2,1)}, /*index=5...) while((s32[]{:T(128)}, f32[24,4096]{1,0:T(8,128)S(1)}, ...), condition=%wide.wide.region_6.7_spmd.clone, body=%wide.wide.region_5.6_spmd.clone.sunk | while | flops 118413576 | bytes 7291664 | solution.py:163
  225.8 8.6 %cosine_convert_fusion.3 = (bf16[2048,256]{1,0:T(8,128)(2,1)S(1)}, bf16[2048,256]{1,0:T(8,128)(2,1)S(1)}) fusion(s32[256]{0:T(256)S(1)} %iota_add_fusion.3), kind=kLoop, calls=%fused_computation.26.clone.clone.1 | loop fusion | flops 8912896 | bytes 2098176 | tf_op jit(solution)/shard_map/convert.1
  236.8 8.6 %cosine_convert_fusion.3 = (bf16[2048,256]{1,0:T(8,128)(2,1)S(1)}, bf16[2048,256]{1,0:T(8,128)(2,1)S(1)}) fusion(s32[256]{0:T(256)S(1)} %iota_add_fusion.3), kind=kLoop, calls=%fused_computation.26.clone.clone.1 | loop fusion | flops 8912896 | bytes 2098176 | tf_op jit(solution)/shard_map/convert.1
  247.9 8.6 %cosine_convert_fusion.3 = (bf16[2048,256]{1,0:T(8,128)(2,1)S(1)}, bf16[2048,256]{1,0:T(8,128)(2,1)S(1)}) fusion(s32[256]{0:T(256)S(1)} %iota_add_fusion.3), kind=kLoop, calls=%fused_computation.26.clone.clone.1 | loop fusion | flops 8912896 | bytes 2098176 | tf_op jit(solution)/shard_map/convert.1
  258.9 8.6 %cosine_convert_fusion.3 = (bf16[2048,256]{1,0:T(8,128)(2,1)S(1)}, bf16[2048,256]{1,0:T(8,128)(2,1)S(1)}) fusion(s32[256]{0:T(256)S(1)} %iota_add_fusion.3), kind=kLoop, calls=%fused_computation.26.clone.clone.1 | loop fusion | flops 8912896 | bytes 2098176 | tf_op jit(solution)/shard_map/convert.1
  270.0 8.6 %cosine_convert_fusion.3 = (bf16[2048,256]{1,0:T(8,128)(2,1)S(1)}, bf16[2048,256]{1,0:T(8,128)(2,1)S(1)}) fusion(s32[256]{0:T(256)S(1)} %iota_add_fusion.3), kind=kLoop, calls=%fused_computation.26.clone.clone.1 | loop fusion | flops 8912896 | bytes 2098176 | tf_op jit(solution)/shard_map/convert.1
  281.0 8.6 %cosine_convert_fusion.3 = (bf16[2048,256]{1,0:T(8,128)(2,1)S(1)}, bf16[2048,256]{1,0:T(8,128)(2,1)S(1)}) fusion(s32[256]{0:T(256)S(1)} %iota_add_fusion.3), kind=kLoop, calls=%fused_computation.26.clone.clone.1 | loop fusion | flops 8912896 | bytes 2098176 | tf_op jit(solution)/shard_map/convert.1
  292.1 8.6 %cosine_convert_fusion.3 = (bf16[2048,256]{1,0:T(8,128)(2,1)S(1)}, bf16[2048,256]{1,0:T(8,128)(2,1)S(1)}) fusion(s32[256]{0:T(256)S(1)} %iota_add_fusion.3), kind=kLoop, calls=%fused_computation.26.clone.clone.1 | loop fusion | flops 8912896 | bytes 2098176 | tf_op jit(solution)/shard_map/convert.1
  303.1 8.6 %cosine_convert_fusion.3 = (bf16[2048,256]{1,0:T(8,128)(2,1)S(1)}, bf16[2048,256]{1,0:T(8,128)(2,1)S(1)}) fusion(s32[256]{0:T(256)S(1)} %iota_add_fusion.3), kind=kLoop, calls=%fused_computation.26.clone.clone.1 | loop fusion | flops 8912896 | bytes 2098176 | tf_op jit(solution)/shard_map/convert.1
  314.2 8.6 %cosine_convert_fusion.3 = (bf16[2048,256]{1,0:T(8,128)(2,1)S(1)}, bf16[2048,256]{1,0:T(8,128)(2,1)S(1)}) fusion(s32[256]{0:T(256)S(1)} %iota_add_fusion.3), kind=kLoop, calls=%fused_computation.26.clone.clone.1 | loop fusion | flops 8912896 | bytes 2098176 | tf_op jit(solution)/shard_map/convert.1
  325.2 8.6 %cosine_convert_fusion.3 = (bf16[2048,256]{1,0:T(8,128)(2,1)S(1)}, bf16[2048,256]{1,0:T(8,128)(2,1)S(1)}) fusion(s32[256]{0:T(256)S(1)} %iota_add_fusion.3), kind=kLoop, calls=%fused_computation.26.clone.clone.1 | loop fusion | flops 8912896 | bytes 2098176 | tf_op jit(solution)/shard_map/convert.1
  336.3 8.6 %cosine_convert_fusion.3 = (bf16[2048,256]{1,0:T(8,128)(2,1)S(1)}, bf16[2048,256]{1,0:T(8,128)(2,1)S(1)}) fusion(s32[256]{0:T(256)S(1)} %iota_add_fusion.3), kind=kLoop, calls=%fused_computation.26.clone.clone.1 | loop fusion | flops 8912896 | bytes 2098176 | tf_op jit(solution)/shard_map/convert.1
  347.3 8.6 %cosine_convert_fusion.3 = (bf16[2048,256]{1,0:T(8,128)(2,1)S(1)}, bf16[2048,256]{1,0:T(8,128)(2,1)S(1)}) fusion(s32[256]{0:T(256)S(1)} %iota_add_fusion.3), kind=kLoop, calls=%fused_computation.26.clone.clone.1 | loop fusion | flops 8912896 | bytes 2098176 | tf_op jit(solution)/shard_map/convert.1
  358.4 8.6 %cosine_convert_fusion.3 = (bf16[2048,256]{1,0:T(8,128)(2,1)S(1)}, bf16[2048,256]{1,0:T(8,128)(2,1)S(1)}) fusion(s32[256]{0:T(256)S(1)} %iota_add_fusion.3), kind=kLoop, calls=%fused_computation.26.clone.clone.1 | loop fusion | flops 8912896 | bytes 2098176 | tf_op jit(solution)/shard_map/convert.1
  369.4 8.6 %cosine_convert_fusion.3 = (bf16[2048,256]{1,0:T(8,128)(2,1)S(1)}, bf16[2048,256]{1,0:T(8,128)(2,1)S(1)}) fusion(s32[256]{0:T(256)S(1)} %iota_add_fusion.3), kind=kLoop, calls=%fused_computation.26.clone.clone.1 | loop fusion | flops 8912896 | bytes 2098176 | tf_op jit(solution)/shard_map/convert.1
  380.5 8.6 %cosine_convert_fusion.3 = (bf16[2048,256]{1,0:T(8,128)(2,1)S(1)}, bf16[2048,256]{1,0:T(8,128)(2,1)S(1)}) fusion(s32[256]{0:T(256)S(1)} %iota_add_fusion.3), kind=kLoop, calls=%fused_computation.26.clone.clone.1 | loop fusion | flops 8912896 | bytes 2098176 | tf_op jit(solution)/shard_map/convert.1
  391.5 8.6 %cosine_convert_fusion.3 = (bf16[2048,256]{1,0:T(8,128)(2,1)S(1)}, bf16[2048,256]{1,0:T(8,128)(2,1)S(1)}) fusion(s32[256]{0:T(256)S(1)} %iota_add_fusion.3), kind=kLoop, calls=%fused_computation.26.clone.clone.1 | loop fusion | flops 8912896 | bytes 2098176 | tf_op jit(solution)/shard_map/convert.1
  411.4 9.1 %all-to-all-done.1 = f32[32,1,384]{2,1,0:T(1,128)S(1)} async-done(((f32[32,1,384]{2,1,0:T(1,128)}), f32[32,1,384]{2,1,0:T(1,128)S(1)}, u32[]{:S(2)}, u32[]{:S(2)}) %all-to-all-start.1) | async-done | bytes 49184 | tf_op jit(solution)/shard_map/all_to_all | solution.py:169
  425.5 39.5 %all_gather.3 = f32[2,1536,64]{2,0,1:T(2,128)S(1)} all-gather(f32[2,96,64]{2,0,1:T(2,128)S(1)} %bitcast.109), channel_id=1, replica_groups=mesh['pair'=32,'day'=16] {'day'}, dimensions={1}, use_global_device_ids=true | all-gather | bytes 835584 | tf_op jit(solution)/shard_map/all_gather | solution.py:171
  475.0 12.5 %while.50 = (s32[]{:T(128)}, f32[256,1024]{1,0:T(8,128)S(1)}, f32[256,1536]{1,0:T(8,128)}, f32[256,1536]{1,0:T(8,128)}, s32[1536,2]{0,1:T(2,128)S(1)}, /*index=5...) while((s32[]{:T(128)}, f32[256,1024]{1,0:T(8,128)S(1)}, f32[256,1536]{1,0:T(8,128)}, ...), condition=%wide.region_9.10_spmd.clone.clone, body=%wide.region_8.9_spmd.clone.clone.sunk | while | flops 3224109056 | bytes 7352501 | solution.py:83
  (164 shorter events, 88.3 us)
Async XLA Ops:
  6.5 1.8 copy-start.8
  6.5 198.8 %all-reduce.2.cloned.1.call-start = ((), (), s32[]{:S(2)}) async-start(), calls=%async_computation.2 | async-start | bytes 1572864 | tf_op jit(solution)/shard_map/psum | solution.py:126
  13.2 1.1 copy-start
  13.2 1.6 copy-start.2
  14.8 1.0 copy-start.7
  14.8 1.8 copy-start.4
  15.8 209.9 %copy-start.5 = (s32[3,8,1]{1,0,2:T(4,128)}, s32[3,8,1]{1,0,2:T(4,128)S(1)}, u32[]{:S(2)}) copy-start(s32[3,8,1]{1,0,2:T(4,128)S(1)} %copy.75) | copy-start | bytes 292
  15.9 209.8 %copy-start.6 = (s32[3,8,1]{1,0,2:T(4,128)}, s32[3,8,1]{1,0,2:T(4,128)S(1)}, u32[]{:S(2)}) copy-start(s32[3,8,1]{1,0,2:T(4,128)S(1)} %copy.76) | copy-start | bytes 292
  207.2 16.8 %all-to-all-start = ((f32[32,1,384]{2,1,0:T(1,128)}), f32[32,1,384]{2,1,0:T(1,128)S(1)}, u32[]{:S(2)}, u32[]{:S(2)}) async-start(f32[32,1,384]{2,1,0:T(1,128)} %reshape.72), calls=%async_computation | async-start | bytes 98304 | tf_op jit(solution)/shard_map/all_to_all | solution.py:130
  407.5 13.0 %all-to-all-start.1 = ((f32[32,1,384]{2,1,0:T(1,128)}), f32[32,1,384]{2,1,0:T(1,128)S(1)}, u32[]{:S(2)}, u32[]{:S(2)}) async-start(f32[32,1,384]{2,1,0:T(1,128)} %reshape.74), calls=%async_computation.1 | async-start | bytes 98304 | tf_op jit(solution)/shard_map/all_to_all | solution.py:169
  464.9 5.7 %copy-start.1 = (f32[2,2,64,1536]{3,2,1,0:T(8,128)S(1)}, f32[2,2,64,1536]{3,2,1,0:T(8,128)}, u32[]{:S(2)}) copy-start(f32[2,2,64,1536]{3,2,1,0:T(8,128)} %copy-done) | copy-start | bytes 4718596
  464.9 5.7 %copy-start.3 = (f32[2,2,64,1536]{3,2,1,0:T(8,128)S(1)}, f32[2,2,64,1536]{3,2,1,0:T(8,128)}, u32[]{:S(2)}) copy-start(f32[2,2,64,1536]{3,2,1,0:T(8,128)} %copy-done.2) | copy-start | bytes 4718596
  473.3 1.7 copy-start.9
  487.6 1.0 copy-start.10
Sparse Core Ops, SparseCore 0:
  15.9 189.3 all-reduce.1
where the time goes:
time: 497 us; the launch traced here: 495 us
  waiting for transfers between devices  207 us (42%)
  other arithmetic  148 us (30%)
  matrix products  45 us (9%)
  blocking collectives  39.5 us (8%)
  local copies, waits for them, and re-layouts  29.9 us (6%)
  between operations  14.4 us (3%)
  starting transfers between devices  11.5 us (2%)
    psum x1, waiting for transfers between devices, body(): total = lax.psum(local_stack, 'day')  189 us
    another operation x16, other arithmetic  138 us
    all_gather x1, blocking collectives, body(): all_pairs = lax.all_gather(spread, 'day', axis=1, tiled=True)  39.5 us
    dot_general x16, matrix products, lag_step(): lax.dot_general(misfit, block_table, (((1,), (1,)), ((), ())), preferred_...  35.5 us
    unnamed x29, local copies, waits for them, and re-layouts  10.3 us
  transfers between devices with their start and end apart: 3, of which 3 were waited for; matrix products, arithmetic and copies ran while one was open for 0% of the time, Pallas kernels for 0%

commit v1 on v0

--- a/solution.py
+++ b/solution.py
@@ -168,7 +168,9 @@
     adjoint_split = adjoint_spec.reshape(per_block, 2, half).transpose(1, 0, 2)
     spread = lax.all_to_all(adjoint_split, "pair", split_axis=2, concat_axis=1, tiled=True)
     start_total = jnp.zeros((flat_spectra.shape[0], station_count), jnp.float32)
-    all_pairs = lax.all_gather(spread, "day", axis=1, tiled=True)
+    all_pairs = jnp.concatenate(
+        lax.all_to_all(jnp.stack([spread] * lax.axis_size("day")), "day", 0, 0), axis=1
+    )
     flat_out = station_terms(start_total, first_rows, second_rows, all_pairs, ordered, day_count)
     return flat_out.reshape(spectra.shape)
 

time: 497 us -> 495 us (level)
  blocking collectives: 39.5 us -> 12.1 us
  waiting for transfers between devices: 207 us -> 224 us
  starting transfers between devices: 11.5 us -> 17.3 us
    all_gather x1 -> x0, blocking collectives: 39.5 us -> none  [body(): all_pairs = lax.all_gather(spread, 'day', axis=1, tiled=True)]
    all_to_all x1, waiting for transfers between devices: 9.09 us -> 25.9 us  [body(): lax.all_to_all(jnp.stack([spread] * lax.axis_size('day')), 'day', 0, 0)]
    all_to_all x0 -> x1, blocking collectives: none -> 12.1 us  [body(): lax.all_to_all(adjoint_split, 'pair', split_axis=2, concat_axis=1, tiled=...]
    all_to_all x1, starting transfers between devices: 3.85 us -> 9.63 us  [body(): lax.all_to_all(jnp.stack([spread] * lax.axis_size('day')), 'day', 0, 0)]
where the time goes in v1:
time: 495 us; the launch traced here: 490 us
  waiting for transfers between devices  224 us (45%)
  other arithmetic  147 us (30%)
  matrix products  45 us (9%)
  local copies, waits for them, and re-layouts  30.2 us (6%)
  starting transfers between devices  17.3 us (3%)
  between operations  14.4 us (3%)
  blocking collectives  12.1 us (2%)
    psum x1, waiting for transfers between devices, body(): total = lax.psum(local_stack, 'day')  189 us
    another operation x16, other arithmetic  138 us
    dot_general x16, matrix products, lag_step(): lax.dot_general(misfit, block_table, (((1,), (1,)), ((), ())), preferred_...  35.5 us
    all_to_all x1, waiting for transfers between devices, body(): lax.all_to_all(jnp.stack([spread] * lax.axis_size('day')), 'day', 0, 0)  25.9 us
    all_to_all x1, blocking collectives, body(): lax.all_to_all(adjoint_split, 'pair', split_axis=2, concat_axis=1, tiled=...  12.1 us
  transfers between devices with their start and end apart: 3, of which 3 were waited for; matrix products, arithmetic and copies ran while one was open for 0% of the time, Pallas kernels for 0%

profile of v1, /device:TPU:1, one launch (start us, length us, event | category | flops | bytes accessed | tf_op | source)
XLA Modules:
  0.0 490.0 jit_solution(11824388512755145945)
XLA Ops:
  16.7 188.6 %all-reduce.2.cloned.1.call-done = f32[2,1536,64]{1,2,0:T(8,128)} async-done(((f32[2,1536,64]{1,2,0:T(8,128)}), f32[2,1536,64]{1,2,0:T(8,128)}) %all-reduce.2.cloned.1.call-update) | async-done | bytes 786448 | tf_op jit(solution)/shard_map/psum | solution.py:126
  207.2 7.7 %all-to-all-start = ((f32[32,1,384]{2,1,0:T(1,128)}), f32[32,1,384]{2,1,0:T(1,128)S(1)}, u32[]{:S(2)}, u32[]{:S(2)}) async-start(f32[32,1,384]{2,1,0:T(1,128)} %reshape.83), calls=%async_computation | async-start | bytes 98304 | tf_op jit(solution)/shard_map/all_to_all | solution.py:130
  214.9 9.1 %all-to-all-done = f32[32,1,384]{2,1,0:T(1,128)S(1)} async-done(((f32[32,1,384]{2,1,0:T(1,128)}), f32[32,1,384]{2,1,0:T(1,128)S(1)}, u32[]{:S(2)}, u32[]{:S(2)}) %all-to-all-start) | async-done | bytes 49184 | tf_op jit(solution)/shard_map/all_to_all | solution.py:130
  225.7 176.8 %while.51 = (s32[]{:T(128)}, f32[24,4096]{1,0:T(8,128)S(1)}, s32[3,8,1]{1,0,2:T(4,128)}, s32[3,8,1]{1,0,2:T(4,128)}, bf16[24,4096]{1,0:T(8,128)(2,1)}, /*index=5...) while((s32[]{:T(128)}, f32[24,4096]{1,0:T(8,128)S(1)}, ...), condition=%wide.wide.region_6.7_spmd.clone, body=%wide.wide.region_5.6_spmd.clone.sunk | while | flops 118413576 | bytes 7291664 | solution.py:163
  225.7 8.6 %cosine_convert_fusion.3 = (bf16[2048,256]{1,0:T(8,128)(2,1)S(1)}, bf16[2048,256]{1,0:T(8,128)(2,1)S(1)}) fusion(s32[256]{0:T(256)S(1)} %iota_add_fusion.3), kind=kLoop, calls=%fused_computation.26.clone.clone.1 | loop fusion | flops 8912896 | bytes 2098176 | tf_op jit(solution)/shard_map/convert.1
  236.8 8.6 %cosine_convert_fusion.3 = (bf16[2048,256]{1,0:T(8,128)(2,1)S(1)}, bf16[2048,256]{1,0:T(8,128)(2,1)S(1)}) fusion(s32[256]{0:T(256)S(1)} %iota_add_fusion.3), kind=kLoop, calls=%fused_computation.26.clone.clone.1 | loop fusion | flops 8912896 | bytes 2098176 | tf_op jit(solution)/shard_map/convert.1
  247.8 8.6 %cosine_convert_fusion.3 = (bf16[2048,256]{1,0:T(8,128)(2,1)S(1)}, bf16[2048,256]{1,0:T(8,128)(2,1)S(1)}) fusion(s32[256]{0:T(256)S(1)} %iota_add_fusion.3), kind=kLoop, calls=%fused_computation.26.clone.clone.1 | loop fusion | flops 8912896 | bytes 2098176 | tf_op jit(solution)/shard_map/convert.1
  258.9 8.6 %cosine_convert_fusion.3 = (bf16[2048,256]{1,0:T(8,128)(2,1)S(1)}, bf16[2048,256]{1,0:T(8,128)(2,1)S(1)}) fusion(s32[256]{0:T(256)S(1)} %iota_add_fusion.3), kind=kLoop, calls=%fused_computation.26.clone.clone.1 | loop fusion | flops 8912896 | bytes 2098176 | tf_op jit(solution)/shard_map/convert.1
  269.9 8.6 %cosine_convert_fusion.3 = (bf16[2048,256]{1,0:T(8,128)(2,1)S(1)}, bf16[2048,256]{1,0:T(8,128)(2,1)S(1)}) fusion(s32[256]{0:T(256)S(1)} %iota_add_fusion.3), kind=kLoop, calls=%fused_computation.26.clone.clone.1 | loop fusion | flops 8912896 | bytes 2098176 | tf_op jit(solution)/shard_map/convert.1
  281.0 8.6 %cosine_convert_fusion.3 = (bf16[2048,256]{1,0:T(8,128)(2,1)S(1)}, bf16[2048,256]{1,0:T(8,128)(2,1)S(1)}) fusion(s32[256]{0:T(256)S(1)} %iota_add_fusion.3), kind=kLoop, calls=%fused_computation.26.clone.clone.1 | loop fusion | flops 8912896 | bytes 2098176 | tf_op jit(solution)/shard_map/convert.1
  292.0 8.6 %cosine_convert_fusion.3 = (bf16[2048,256]{1,0:T(8,128)(2,1)S(1)}, bf16[2048,256]{1,0:T(8,128)(2,1)S(1)}) fusion(s32[256]{0:T(256)S(1)} %iota_add_fusion.3), kind=kLoop, calls=%fused_computation.26.clone.clone.1 | loop fusion | flops 8912896 | bytes 2098176 | tf_op jit(solution)/shard_map/convert.1
  303.1 8.6 %cosine_convert_fusion.3 = (bf16[2048,256]{1,0:T(8,128)(2,1)S(1)}, bf16[2048,256]{1,0:T(8,128)(2,1)S(1)}) fusion(s32[256]{0:T(256)S(1)} %iota_add_fusion.3), kind=kLoop, calls=%fused_computation.26.clone.clone.1 | loop fusion | flops 8912896 | bytes 2098176 | tf_op jit(solution)/shard_map/convert.1
  314.1 8.6 %cosine_convert_fusion.3 = (bf16[2048,256]{1,0:T(8,128)(2,1)S(1)}, bf16[2048,256]{1,0:T(8,128)(2,1)S(1)}) fusion(s32[256]{0:T(256)S(1)} %iota_add_fusion.3), kind=kLoop, calls=%fused_computation.26.clone.clone.1 | loop fusion | flops 8912896 | bytes 2098176 | tf_op jit(solution)/shard_map/convert.1
  325.2 8.6 %cosine_convert_fusion.3 = (bf16[2048,256]{1,0:T(8,128)(2,1)S(1)}, bf16[2048,256]{1,0:T(8,128)(2,1)S(1)}) fusion(s32[256]{0:T(256)S(1)} %iota_add_fusion.3), kind=kLoop, calls=%fused_computation.26.clone.clone.1 | loop fusion | flops 8912896 | bytes 2098176 | tf_op jit(solution)/shard_map/convert.1
  336.2 8.6 %cosine_convert_fusion.3 = (bf16[2048,256]{1,0:T(8,128)(2,1)S(1)}, bf16[2048,256]{1,0:T(8,128)(2,1)S(1)}) fusion(s32[256]{0:T(256)S(1)} %iota_add_fusion.3), kind=kLoop, calls=%fused_computation.26.clone.clone.1 | loop fusion | flops 8912896 | bytes 2098176 | tf_op jit(solution)/shard_map/convert.1
  347.3 8.6 %cosine_convert_fusion.3 = (bf16[2048,256]{1,0:T(8,128)(2,1)S(1)}, bf16[2048,256]{1,0:T(8,128)(2,1)S(1)}) fusion(s32[256]{0:T(256)S(1)} %iota_add_fusion.3), kind=kLoop, calls=%fused_computation.26.clone.clone.1 | loop fusion | flops 8912896 | bytes 2098176 | tf_op jit(solution)/shard_map/convert.1
  358.3 8.6 %cosine_convert_fusion.3 = (bf16[2048,256]{1,0:T(8,128)(2,1)S(1)}, bf16[2048,256]{1,0:T(8,128)(2,1)S(1)}) fusion(s32[256]{0:T(256)S(1)} %iota_add_fusion.3), kind=kLoop, calls=%fused_computation.26.clone.clone.1 | loop fusion | flops 8912896 | bytes 2098176 | tf_op jit(solution)/shard_map/convert.1
  369.4 8.6 %cosine_convert_fusion.3 = (bf16[2048,256]{1,0:T(8,128)(2,1)S(1)}, bf16[2048,256]{1,0:T(8,128)(2,1)S(1)}) fusion(s32[256]{0:T(256)S(1)} %iota_add_fusion.3), kind=kLoop, calls=%fused_computation.26.clone.clone.1 | loop fusion | flops 8912896 | bytes 2098176 | tf_op jit(solution)/shard_map/convert.1
  380.4 8.6 %cosine_convert_fusion.3 = (bf16[2048,256]{1,0:T(8,128)(2,1)S(1)}, bf16[2048,256]{1,0:T(8,128)(2,1)S(1)}) fusion(s32[256]{0:T(256)S(1)} %iota_add_fusion.3), kind=kLoop, calls=%fused_computation.26.clone.clone.1 | loop fusion | flops 8912896 | bytes 2098176 | tf_op jit(solution)/shard_map/convert.1
  391.5 8.6 %cosine_convert_fusion.3 = (bf16[2048,256]{1,0:T(8,128)(2,1)S(1)}, bf16[2048,256]{1,0:T(8,128)(2,1)S(1)}) fusion(s32[256]{0:T(256)S(1)} %iota_add_fusion.3), kind=kLoop, calls=%fused_computation.26.clone.clone.1 | loop fusion | flops 8912896 | bytes 2098176 | tf_op jit(solution)/shard_map/convert.1
  406.9 12.1 %all_to_all.35 = f32[32,1,384]{2,1,0:T(1,128)S(1)} all-to-all(f32[32,1,384]{2,1,0:T(1,128)S(1)} %reshape.85), channel_id=1, replica_groups=mesh['pair'=32,'day'=16] {'pair'}, dimensions={0} | all-to-all | bytes 98304 | tf_op jit(solution)/shard_map/all_to_all | solution.py:169
  425.2 9.6 %all-to-all-start.2 = ((f32[16,2,96,64]{2,3,1,0:T(8,128)}), f32[16,2,96,64]{2,3,1,0:T(8,128)S(1)}, u32[]{:S(2)}, u32[]{:S(2)}) async-start(f32[16,2,96,64]{2,3,1,0:T(8,128)} %stack.18), calls=%async_computation.2 | async-start | bytes 2097152 | tf_op jit(solution)/shard_map/all_to_all | solution.py:172
  434.8 25.9 %all-to-all-done.2 = f32[16,2,96,64]{2,3,1,0:T(8,128)S(1)} async-done(((f32[16,2,96,64]{2,3,1,0:T(8,128)}), f32[16,2,96,64]{2,3,1,0:T(8,128)S(1)}, u32[]{:S(2)}, u32[]{:S(2)}) %all-to-all-start.2) | async-done | bytes 786464 | tf_op jit(solution)/shard_map/all_to_all | solution.py:172
  469.6 12.5 %while.50 = (s32[]{:T(128)}, f32[256,1024]{1,0:T(8,128)S(1)}, f32[256,1536]{1,0:T(8,128)}, f32[256,1536]{1,0:T(8,128)}, s32[1536,2]{0,1:T(2,128)S(1)}, /*index=5...) while((s32[]{:T(128)}, f32[256,1024]{1,0:T(8,128)S(1)}, f32[256,1536]{1,0:T(8,128)}, ...), condition=%wide.region_9.10_spmd.clone.clone, body=%wide.region_8.9_spmd.clone.clone.sunk | while | flops 3224109056 | bytes 7352501 | solution.py:83
  (166 shorter events, 88.3 us)
Async XLA Ops:
  6.5 1.8 copy-start.8
  6.5 198.8 %all-reduce.2.cloned.1.call-start = ((), (), s32[]{:S(2)}) async-start(), calls=%async_computation.3 | async-start | bytes 1572864 | tf_op jit(solution)/shard_map/psum | solution.py:126
  13.2 1.1 copy-start
  13.2 1.6 copy-start.2
  14.8 1.0 copy-start.7
  14.8 1.8 copy-start.4
  15.8 209.9 %copy-start.5 = (s32[3,8,1]{1,0,2:T(4,128)}, s32[3,8,1]{1,0,2:T(4,128)S(1)}, u32[]{:S(2)}) copy-start(s32[3,8,1]{1,0,2:T(4,128)S(1)} %copy.72) | copy-start | bytes 292
  15.9 209.8 %copy-start.6 = (s32[3,8,1]{1,0,2:T(4,128)}, s32[3,8,1]{1,0,2:T(4,128)S(1)}, u32[]{:S(2)}) copy-start(s32[3,8,1]{1,0,2:T(4,128)S(1)} %copy.73) | copy-start | bytes 292
  207.2 16.8 %all-to-all-start = ((f32[32,1,384]{2,1,0:T(1,128)}), f32[32,1,384]{2,1,0:T(1,128)S(1)}, u32[]{:S(2)}, u32[]{:S(2)}) async-start(f32[32,1,384]{2,1,0:T(1,128)} %reshape.83), calls=%async_computation | async-start | bytes 98304 | tf_op jit(solution)/shard_map/all_to_all | solution.py:130
  425.2 35.5 %all-to-all-start.2 = ((f32[16,2,96,64]{2,3,1,0:T(8,128)}), f32[16,2,96,64]{2,3,1,0:T(8,128)S(1)}, u32[]{:S(2)}, u32[]{:S(2)}) async-start(f32[16,2,96,64]{2,3,1,0:T(8,128)} %stack.18), calls=%async_computation.2 | async-start | bytes 2097152 | tf_op jit(solution)/shard_map/all_to_all | solution.py:172
  462.3 3.9 copy-start.1
  462.3 3.9 copy-start.3
  467.9 1.7 copy-start.9
  482.2 1.0 copy-start.10
Sparse Core Ops, SparseCore 0:
  15.9 189.3 all-reduce.1
